TPU v7x, 32 devices: a whole 2x2x4 slice. The times are simulated.
32 devices in a mesh: rec: 2 (over y), leaf: 4 (over z), rhs: 2 (over x), pan: 2 (over core).
Axes of the slice: x: 2, y: 2, z: 4, core: 2. Of those that a mesh axis runs over, the one named last changes fastest.
Arguments:
- bottom_source: bfloat16 [32768, 256], P(('rec', 'leaf', 'rhs', 'pan')), parts along dimension 0, may hold values from -6 to 6
- bottom_inverse: bfloat16 [32768, 1024], P(('rec', 'leaf', 'rhs', 'pan')), parts along dimension 0, as said below
- bottom_update: bfloat16 [4096, 1024], P(('rec', 'leaf', 'rhs', 'pan')), parts along dimension 0, may hold values from -0.0625 to 0.0625
- bottom_sensitivity: bfloat16 [1024, 16384], P('rec', ('leaf', 'rhs', 'pan')), parts along dimension 0, may hold values from -0.03125 to 0.03125
- bottom_order: int32 [16, 1024], P(('leaf', 'rhs', 'pan')), may hold values from 0 to 1023, each once within a row
- bottom_extent: int32 [16], P(('leaf', 'rhs', 'pan')), may hold values from 384 to 1024, as said below
- bottom_targets: int32 [16, 128], P(('leaf', 'rhs', 'pan')), may hold values from 0 to 255, as said below
- upper_source: bfloat16 [3584, 256], P(('rec', 'leaf'), ('rhs', 'pan')), parts along dimension 0, may hold values from -6 to 6
- upper_inverse: bfloat16 [3584, 256], P(('rec', 'leaf')), parts along dimension 0, as said below
- upper_update: bfloat16 [256, 1536], P('rec', 'leaf'), parts along dimension 0, may hold values from -0.25 to 0.25
- upper_targets: int32 [6, 128], replicated, may hold values from 0 to 255, as said below
Outputs:
- adjoint: bfloat16 [32768, 256], P(('rec', 'leaf', 'rhs', 'pan')), parts along dimension 0
- gradient: float32 [1024, 256], P(('rec', 'leaf', 'rhs', 'pan')), parts along dimension 0
There are 2 independent parts, one for each index of `rec`. A program takes and returns all parts, laid end to end along the dimension named above; an argument that names none is the same for every part. Nothing has to cross between parts.
Inputs may be any that keep to these rules, and one draw needn't show every extreme that they name: `bottom_inverse`: lower triangular, with its diagonal between 0.6 and 1.4. `upper_inverse`: lower triangular in each front's row order, with its diagonal between 0.6 and 1.4. `bottom_extent`: a multiple of 128; some front uses all 1024 rows. `bottom_targets`: the rows of one front go to distinct rows. `upper_targets`: the rows of one front go to distinct rows.
All inputs are finite; a program needn't handle non-finite values.
Results may differ from a plain program's by a relative error of at most 0.0058.
Values may be sent and summed in bfloat16 or wider, within the bound.
A program may use at most 64 MiB of HBM per device.

v0:
```python
import jax
import jax.numpy as jnp
from jax import lax
from jax.sharding import PartitionSpec as P


def partner(value, axis, apart):
    mask = 2**apart
    pairs = [(source, source ^ mask) for source in range(lax.axis_size(axis))]
    return lax.ppermute(value, axis, pairs)


def climb_sum(values, bit_count):
    for bit_index in range(bit_count):
        values = values + partner(values, "leaf", bit_index)
    return values


def descend_sum(values, bit_count):
    for bit_index in range(bit_count):
        values = values + partner(values, "leaf", bit_index)
    return values


def shards(
    bottom_source,
    bottom_inverse,
    bottom_update,
    bottom_sensitivity,
    bottom_order,
    bottom_extent,
    bottom_targets,
    upper_source,
    upper_inverse,
    upper_update,
    upper_targets,
):
    leaves = lax.axis_size("leaf")
    depth = leaves.bit_length() - 1
    leaf_place = lax.axis_index("leaf")
    front_rows = bottom_inverse.shape[0]
    front_size = upper_inverse.shape[1]
    order_rows = bottom_order[0]
    row_mask = (jnp.arange(front_rows, dtype=jnp.int32) < bottom_extent[0]).astype(jnp.bfloat16)[
        :, None
    ]
    ordered = bottom_source[order_rows] * row_mask
    solved = (
        jnp.dot(bottom_inverse, ordered, preferred_element_type=jnp.float32) * row_mask
    ).astype(jnp.bfloat16)
    contrib = jnp.dot(bottom_update, solved, preferred_element_type=jnp.float32)
    spread = (
        jnp.zeros((front_size, contrib.shape[1]), jnp.float32).at[bottom_targets[0]].set(contrib)
    )
    summed = lax.psum(spread, ("rhs", "pan"))
    loads = lax.all_gather(upper_source, ("rhs", "pan"), axis=1, tiled=True)
    column_count = summed.shape[1]
    front_input = (loads[0:front_size].astype(jnp.float32) - summed).astype(jnp.bfloat16)
    solved_upper = []
    for height in range(depth + 1):
        row_count = front_size >> height
        offset = 2 * front_size - (2 * front_size >> height)
        inverse_now = upper_inverse[offset : offset + row_count]
        solved_front = jnp.dot(inverse_now, front_input, preferred_element_type=jnp.float32).astype(
            jnp.bfloat16
        )
        solved_upper.append(solved_front)
        if height < depth:
            update_now = upper_update[:, offset : offset + row_count]
            lifted = jnp.dot(update_now, solved_front, preferred_element_type=jnp.float32)
            map_row = 2 * leaves - (2 * leaves >> height) + leaf_place // (1 << height)
            targets = lax.dynamic_slice_in_dim(upper_targets, map_row, 1, 0)[0]
            partial_input = (
                jnp.zeros((front_size, column_count), jnp.float32).at[targets].set(-lifted)
            )
            parent_rows = front_size >> height + 1
            parent_offset = 2 * front_size - (2 * front_size >> height + 1)
            parent_place = leaf_place % (2 << height) * parent_rows
            own_load = loads[parent_offset : parent_offset + parent_rows].astype(jnp.float32)
            current = lax.dynamic_slice_in_dim(partial_input, parent_place, parent_rows, 0)
            partial_input = lax.dynamic_update_slice_in_dim(
                partial_input, current + own_load, parent_place, 0
            )
            front_input = climb_sum(partial_input, height + 1).astype(jnp.bfloat16)
    back_rows = None
    for height in range(depth, -1, -1):
        row_count = front_size >> height
        offset = 2 * front_size - (2 * front_size >> height)
        inverse_now = upper_inverse[offset : offset + row_count]
        if height == depth:
            residue = solved_upper[height]
        else:
            map_row = 2 * leaves - (2 * leaves >> height) + leaf_place // (1 << height)
            targets = lax.dynamic_slice_in_dim(upper_targets, map_row, 1, 0)[0]
            picked = back_rows[targets]
            update_now = upper_update[:, offset : offset + row_count]
            coupled = jnp.einsum(
                "rj,rc->jc", update_now, picked, preferred_element_type=jnp.float32
            )
            residue = (solved_upper[height].astype(jnp.float32) - coupled).astype(jnp.bfloat16)
        partial_back = jnp.einsum(
            "ij,ic->jc", inverse_now, residue, preferred_element_type=jnp.float32
        )
        back_rows = descend_sum(partial_back, height).astype(jnp.bfloat16)
    picked_root = back_rows[bottom_targets[0]]
    coupled_root = jnp.einsum(
        "rj,rc->jc", bottom_update, picked_root, preferred_element_type=jnp.float32
    )
    bottom_residue = ((solved.astype(jnp.float32) - coupled_root) * row_mask).astype(jnp.bfloat16)
    bottom_back = (
        jnp.einsum("ij,ic->jc", bottom_inverse, bottom_residue, preferred_element_type=jnp.float32)
        * row_mask
    ).astype(jnp.bfloat16)
    adjoint = jnp.zeros_like(bottom_back).at[order_rows].set(bottom_back)
    gradient = lax.psum_scatter(
        -jnp.dot(bottom_sensitivity, adjoint, preferred_element_type=jnp.float32),
        ("leaf", "rhs", "pan"),
        scatter_dimension=0,
        tiled=True,
    )
    return (adjoint, gradient)


def solution(mesh):
    placed = (
        P(("rec", "leaf", "rhs", "pan"), None),
        P(("rec", "leaf", "rhs", "pan"), None),
        P(("rec", "leaf", "rhs", "pan"), None),
        P("rec", ("leaf", "rhs", "pan")),
        P(("leaf", "rhs", "pan"), None),
        P(("leaf", "rhs", "pan")),
        P(("leaf", "rhs", "pan"), None),
        P(("rec", "leaf"), ("rhs", "pan")),
        P(("rec", "leaf"), None),
        P("rec", "leaf"),
        P(),
    )
    return jax.shard_map(
        shards,
        mesh=mesh,
        in_specs=placed,
        out_specs=(P(("rec", "leaf", "rhs", "pan"), None), P(("rec", "leaf", "rhs", "pan"), None)),
        check_vma=False,
    )
```

profile of v0, /device:TPU:0, one launch (start us, length us, event | category | flops | bytes accessed | tf_op | source)
XLA Modules:
  0.0 189.3 jit_solution(15696807839329698646)
XLA Ops:
  9.4 4.6 %gather_fusion = bf16[1024,256]{1,0:T(8,128)(2,1)S(1)} fusion(bf16[1024,256]{1,0:T(8,128)(2,1)} %param.11, s32[1024]{0:T(1024)S(1)} %broadcast_clamp_fusion), kind=kCustom, calls=%fused_computation | custom fusion | bytes 1052672 | tf_op jit(solution)/shard_map/gather | solution.py:47
  14.0 1.0 fusion.3
  15.0 0.8 copy-done.3
  16.2 1.7 scatter_custom_fusion
  18.0 7.2 %all_gather.3 = bf16[448,256]{0,1:T(8,128)(2,1)S(1)} all-gather(bf16[448,64]{0,1:T(8,128)(2,1)S(1)} %copy-done.7), channel_id=1, replica_groups=mesh['rec'=2,'leaf'=4,'rhs'=2,'pan'=2] {'rhs','pan'}, dimensions={1}, use_global_device_ids=true | all-gather | bytes 286720 | tf_op jit(solution)/shard_map/all_gather | solution.py:56
  25.5 0.8 fusion.45
  26.3 26.5 %all-reduce.2.cloned.1.call-done = f32[256,256]{1,0:T(8,128)} async-done(((f32[256,256]{1,0:T(8,128)}), f32[256,256]{1,0:T(8,128)}) %all-reduce.2.cloned.1.call-update) | async-done | bytes 262160 | tf_op jit(solution)/shard_map/psum | solution.py:55
  52.8 1.2 convolution_convert_fusion.1
  54.2 1.1 scatter_custom_fusion.1
  55.4 1.6 collective-permute-start
  57.0 5.1 %collective-permute-done = f32[256,256]{1,0:T(8,128)S(1)} collective-permute-done((f32[256,256]{1,0:T(8,128)S(1)}, f32[256,256]{1,0:T(8,128)S(1)}, u32[]{:S(2)}, u32[]{:S(2)}) %collective-permute-start) | collective-permute-done | bytes 262176 | tf_op jit(solution)/shard_map/ppermute | solution.py:10
  62.6 1.1 scatter_custom_fusion.2
  63.7 1.8 collective-permute-start.1
  65.5 4.6 %collective-permute-done.1 = f32[256,256]{1,0:T(8,128)S(1)} collective-permute-done((f32[256,256]{1,0:T(8,128)S(1)}, f32[256,256]{1,0:T(8,128)S(1)}, u32[]{:S(2)}, u32[]{:S(2)}) %collective-permute-start.1) | collective-permute-done | bytes 262176 | tf_op jit(solution)/shard_map/ppermute | solution.py:10
  70.2 3.3 %collective-permute-start.2 = (f32[256,256]{1,0:T(8,128)S(1)}, f32[256,256]{1,0:T(8,128)S(1)}, u32[]{:S(2)}, u32[]{:S(2)}) collective-permute-start(f32[256,256]{1,0:T(8,128)S(1)} %add.117), channel_id=1, source_target_pairs={{0,8},{4,12},{8,0},{12,4},{1,9},{5,13},{9,1},{13,5},{2,10},{6,14},... | collective-permute-start | bytes 786440 | tf_op jit(solution)/shard_map/ppermute | solution.py:10
  73.5 8.1 %collective-permute-done.2 = f32[256,256]{1,0:T(8,128)S(1)} collective-permute-done((f32[256,256]{1,0:T(8,128)S(1)}, f32[256,256]{1,0:T(8,128)S(1)}, u32[]{:S(2)}, u32[]{:S(2)}) %collective-permute-start.2) | collective-permute-done | bytes 262176 | tf_op jit(solution)/shard_map/ppermute | solution.py:10
  82.0 0.8 collective-permute-start.3
  82.8 5.6 %collective-permute-done.3 = f32[256,256]{0,1:T(8,128)S(1)} collective-permute-done((f32[256,256]{0,1:T(8,128)S(1)}, f32[256,256]{0,1:T(8,128)S(1)}, u32[]{:S(2)}, u32[]{:S(2)}) %collective-permute-start.3) | collective-permute-done | bytes 262176 | tf_op jit(solution)/shard_map/ppermute | solution.py:10
  88.5 2.8 %collective-permute-start.4 = (f32[256,256]{0,1:T(8,128)S(1)}, f32[256,256]{0,1:T(8,128)S(1)}, u32[]{:S(2)}, u32[]{:S(2)}) collective-permute-start(f32[256,256]{0,1:T(8,128)S(1)} %add.119), channel_id=1, source_target_pairs={{0,8},{4,12},{8,0},{12,4},{1,9},{5,13},{9,1},{13,5},{2,10},{6,14},... | collective-permute-start | bytes 786440 | tf_op jit(solution)/shard_map/ppermute | solution.py:10
  91.3 9.9 %collective-permute-done.4 = f32[256,256]{0,1:T(8,128)S(1)} collective-permute-done((f32[256,256]{0,1:T(8,128)S(1)}, f32[256,256]{0,1:T(8,128)S(1)}, u32[]{:S(2)}, u32[]{:S(2)}) %collective-permute-start.4) | collective-permute-done | bytes 262176 | tf_op jit(solution)/shard_map/ppermute | solution.py:10
  101.3 0.8 gather_fusion.1
  102.2 1.1 convolution_bitcast_fusion
  103.3 0.8 collective-permute-start.5
  104.1 6.5 %collective-permute-done.5 = f32[256,256]{0,1:T(8,128)S(1)} collective-permute-done((f32[256,256]{0,1:T(8,128)S(1)}, f32[256,256]{0,1:T(8,128)S(1)}, u32[]{:S(2)}, u32[]{:S(2)}) %collective-permute-start.5) | collective-permute-done | bytes 262176 | tf_op jit(solution)/shard_map/ppermute | solution.py:10
  110.8 0.8 gather_fusion.2
  111.6 1.2 fusion.7
  112.9 0.8 gather_fusion.3
  113.8 1.8 fusion.4
  115.8 5.1 %scatter_custom_fusion.3 = bf16[1024,256]{1,0:T(8,128)(2,1)S(1)} fusion(s32[1024]{0:T(1024)S(1)} %bitcast.59, bf16[1024,256]{1,0:T(8,128)(2,1)S(1)} %copy.36, bf16[]{:T(256)} %constant.56.clone.1), kind=kCustom, calls=%fused_computation.42 | custom fusion | bytes 524290 | tf_op jit(solution)/shard_map/scatter | solution.py:114
  120.9 1.9 %fusion.5 = f32[512,256]{0,1:T(8,128)S(1)} fusion(bf16[1024,256]{1,0:T(8,128)(2,1)S(1)} %scatter_custom_fusion.3, bf16[512,1024]{1,0:T(8,128)(2,1)} %param.14), kind=kOutput, calls=%fused_computation.17 | convolution fusion | flops 268566528 | bytes 2097152 | tf_op jit(solution)/shard_map/dot_general | solution.py:116
  122.8 1.0 copy.38
  123.9 58.6 %reduce-scatter.4.cloned.1.call-done = f32[32,256]{1,0:T(8,128)} async-done(((f32[512,256]{1,0:T(8,128)}), f32[32,256]{1,0:T(8,128)}) %reduce-scatter.4.cloned.1.call-update) | async-done | bytes 32784
  (50 shorter events, 4.1 us)
Async XLA Ops:
  7.2 6.8 %copy-start = (bf16[1024,1024]{1,0:T(8,128)(2,1)S(1)}, bf16[1024,1024]{1,0:T(8,128)(2,1)}, u32[]{:S(2)}) copy-start(bf16[1024,1024]{1,0:T(8,128)(2,1)} %param.12) | copy-start | bytes 6291460
  7.2 45.6 %all-reduce.2.cloned.1.call-start = ((), (), s32[]{:S(2)}) async-start(), calls=%async_computation.1 | async-start | bytes 524288 | tf_op jit(solution)/shard_map/psum | solution.py:55
  14.0 1.8 copy-start.6
  14.0 4.0 %copy-start.7 = (bf16[448,64]{0,1:T(8,128)(2,1)S(1)}, bf16[448,64]{0,1:T(8,128)(2,1)}, u32[]{:S(2)}) copy-start(bf16[448,64]{0,1:T(8,128)(2,1)} %param.18) | copy-start | bytes 172036
  15.0 0.8 copy-start.3
  15.8 36.9 %copy-start.2 = (bf16[448,256]{1,0:T(8,128)(2,1)S(1)}, bf16[448,256]{1,0:T(8,128)(2,1)}, u32[]{:S(2)}) copy-start(bf16[448,256]{1,0:T(8,128)(2,1)} %param.19) | copy-start | bytes 688132
  15.8 38.1 %copy-start.5 = (bf16[128,384]{1,0:T(8,128)(2,1)S(1)}, bf16[128,384]{1,0:T(8,128)(2,1)}, u32[]{:S(2)}) copy-start(bf16[128,384]{1,0:T(8,128)(2,1)} %param.20) | copy-start | bytes 294916
  17.9 164.5 %reduce-scatter.4.cloned.1.call-start = ((), (), s32[]{:S(2)}) async-start(), calls=%async_computation.2 | async-start | bytes 557056
  55.4 6.7 %collective-permute-start = (f32[256,256]{1,0:T(8,128)S(1)}, f32[256,256]{1,0:T(8,128)S(1)}, u32[]{:S(2)}, u32[]{:S(2)}) collective-permute-start(f32[256,256]{1,0:T(8,128)S(1)} %add_dynamic-update-slice_fusion), channel_id=1, source_target_pairs={{0,4},{4,0},{8,12},{12,8},{1,5},{5,1},{9,13},{13,9},{2,6},{6,2},{1... | collective-permute-start | bytes 786440 | tf_op jit(solution)/shard_map/ppermute | solution.py:10
  63.7 6.4 %collective-permute-start.1 = (f32[256,256]{1,0:T(8,128)S(1)}, f32[256,256]{1,0:T(8,128)S(1)}, u32[]{:S(2)}, u32[]{:S(2)}) collective-permute-start(f32[256,256]{1,0:T(8,128)S(1)} %add_dynamic-update-slice_fusion.1), channel_id=1, source_target_pairs={{0,4},{4,0},{8,12},{12,8},{1,5},{5,1},{9,13},{13,9},{2,6},{6,2},{1... | collective-permute-start | bytes 786440 | tf_op jit(solution)/shard_map/ppermute | solution.py:10
  70.2 11.4 %collective-permute-start.2 = (f32[256,256]{1,0:T(8,128)S(1)}, f32[256,256]{1,0:T(8,128)S(1)}, u32[]{:S(2)}, u32[]{:S(2)}) collective-permute-start(f32[256,256]{1,0:T(8,128)S(1)} %add.117), channel_id=1, source_target_pairs={{0,8},{4,12},{8,0},{12,4},{1,9},{5,13},{9,1},{13,5},{2,10},{6,14},... | collective-permute-start | bytes 786440 | tf_op jit(solution)/shard_map/ppermute | solution.py:10
  82.0 6.4 %collective-permute-start.3 = (f32[256,256]{0,1:T(8,128)S(1)}, f32[256,256]{0,1:T(8,128)S(1)}, u32[]{:S(2)}, u32[]{:S(2)}) collective-permute-start(f32[256,256]{0,1:T(8,128)S(1)} %convolution_bitcast_fusion.1), channel_id=1, source_target_pairs={{0,4},{4,0},{8,12},{12,8},{1,5},{5,1},{9,13},{13,9},{2,6},{6,2},{1... | collective-permute-start | bytes 786440 | tf_op jit(solution)/shard_map/ppermute | solution.py:10
  88.5 12.7 %collective-permute-start.4 = (f32[256,256]{0,1:T(8,128)S(1)}, f32[256,256]{0,1:T(8,128)S(1)}, u32[]{:S(2)}, u32[]{:S(2)}) collective-permute-start(f32[256,256]{0,1:T(8,128)S(1)} %add.119), channel_id=1, source_target_pairs={{0,8},{4,12},{8,0},{12,4},{1,9},{5,13},{9,1},{13,5},{2,10},{6,14},... | collective-permute-start | bytes 786440 | tf_op jit(solution)/shard_map/ppermute | solution.py:10
  101.2 12.6 %copy-start.4 = (bf16[256,1024]{1,0:T(8,128)(2,1)S(1)}, bf16[256,1024]{1,0:T(8,128)(2,1)}, u32[]{:S(2)}) copy-start(bf16[256,1024]{1,0:T(8,128)(2,1)} %copy-done.3) | copy-start | bytes 1572868
  103.3 7.3 %collective-permute-start.5 = (f32[256,256]{0,1:T(8,128)S(1)}, f32[256,256]{0,1:T(8,128)S(1)}, u32[]{:S(2)}, u32[]{:S(2)}) collective-permute-start(f32[256,256]{0,1:T(8,128)S(1)} %convolution_bitcast_fusion), channel_id=1, source_target_pairs={{0,4},{4,0},{8,12},{12,8},{1,5},{5,1},{9,13},{13,9},{2,6},{6,2},{1... | collective-permute-start | bytes 786440 | tf_op jit(solution)/shard_map/ppermute | solution.py:10
  120.9 61.5 %copy-start.1 = (bf16[1024,256]{1,0:T(8,128)(2,1)}, bf16[1024,256]{1,0:T(8,128)(2,1)S(1)}, u32[]{:S(2)}) copy-start(bf16[1024,256]{1,0:T(8,128)(2,1)S(1)} %scatter_custom_fusion.3) | copy-start | bytes 1572868
Sparse Core Ops, SparseCore 0:
  18.1 34.6 all-reduce.1
  124.0 58.4 reduce-scatter.3
where the time goes:
time: 190 us; the launch traced here: 189 us
  waiting for transfers between devices  125 us (66%)
  local copies, waits for them, and re-layouts  19 us (10%)
  between operations  15.2 us (8%)
  starting transfers between devices  11.1 us (6%)
  matrix products  9.46 us (5%)
  blocking collectives  7.19 us (4%)
  other arithmetic  2.34 us (1%)
    unnamed x3, waiting for transfers between devices  58.6 us
    ppermute x6, waiting for transfers between devices, partner(): return lax.ppermute(value, axis, pairs)  39.9 us
    psum x1, waiting for transfers between devices, shards(): summed = lax.psum(spread, ('rhs', 'pan'))  26.5 us
    ppermute x6, starting transfers between devices, partner(): return lax.ppermute(value, axis, pairs)  11 us
    all_gather x1, blocking collectives, shards(): loads = lax.all_gather(upper_source, ('rhs', 'pan'), axis=1, tiled=True)  7.19 us
    scatter x1, local copies, waits for them, and re-layouts, shards(): adjoint = jnp.zeros_like(bottom_back).at[order_rows].set(bottom_back)  5.07 us
    gather x1, local copies, waits for them, and re-layouts, shards(): ordered = bottom_source[order_rows] * row_mask  4.57 us
  transfers between devices with their start and end apart: 8, of which 8 were waited for; matrix products, arithmetic and copies ran while one was open for 1% of the time, Pallas kernels for 0%

commit v1 on v0

--- a/solution.py
+++ b/solution.py
@@ -52,7 +52,7 @@
     spread = (
         jnp.zeros((front_size, contrib.shape[1]), jnp.float32).at[bottom_targets[0]].set(contrib)
     )
-    summed = lax.psum(spread, ("rhs", "pan"))
+    summed = lax.psum(lax.psum(spread, "pan"), "rhs")
     loads = lax.all_gather(upper_source, ("rhs", "pan"), axis=1, tiled=True)
     column_count = summed.shape[1]
     front_input = (loads[0:front_size].astype(jnp.float32) - summed).astype(jnp.bfloat16)

time: 190 us -> 205 us (1.079)
  waiting for transfers between devices: 125 us -> 143 us
    psum x1 -> x2, waiting for transfers between devices: 26.5 us -> 40.7 us  [shards(): summed = lax.psum(lax.psum(spread, 'pan'), 'rhs')]
    ppermute x6, waiting for transfers between devices: 39.9 us -> 45.2 us  [partner(): return lax.ppermute(value, axis, pairs)]
    unnamed x3 -> x4, waiting for transfers between devices: 58.6 us -> 57 us
  transfers between devices with their start and end apart: 8 -> 9, of which waited for: 8 -> 9; matrix products, arithmetic and copies ran while one was open for 1% -> 1% of each run, Pallas kernels for 0% -> 0%
where the time goes in v1:
time: 205 us; the launch traced here: 204 us
  waiting for transfers between devices  143 us (70%)
  local copies, waits for them, and re-layouts  20 us (10%)
  between operations  14.9 us (7%)
  starting transfers between devices  9.57 us (5%)
  matrix products  8.66 us (4%)
  blocking collectives  5.98 us (3%)
  other arithmetic  2.35 us (1%)
    unnamed x4, waiting for transfers between devices  57 us
    ppermute x6, waiting for transfers between devices, partner(): return lax.ppermute(value, axis, pairs)  45.2 us
    psum x2, waiting for transfers between devices, shards(): summed = lax.psum(lax.psum(spread, 'pan'), 'rhs')  40.7 us
    ppermute x6, starting transfers between devices, partner(): return lax.ppermute(value, axis, pairs)  9.45 us
    all_gather x1, blocking collectives, shards(): loads = lax.all_gather(upper_source, ('rhs', 'pan'), axis=1, tiled=True)  5.98 us
    scatter x1, local copies, waits for them, and re-layouts, shards(): adjoint = jnp.zeros_like(bottom_back).at[order_rows].set(bottom_back)  5.07 us
    gather x1, local copies, waits for them, and re-layouts, shards(): ordered = bottom_source[order_rows] * row_mask  4.57 us
  transfers between devices with their start and end apart: 9, of which 9 were waited for; matrix products, arithmetic and copies ran while one was open for 1% of the time, Pallas kernels for 0%

profile of v1, /device:TPU:0, one launch (start us, length us, event | category | flops | bytes accessed | tf_op | source)
XLA Modules:
  0.0 204.5 jit_solution(14554729601256036595)
XLA Ops:
  8.7 0.7 compare_select_fusion
  9.4 4.6 %gather_fusion = bf16[1024,256]{1,0:T(8,128)(2,1)S(1)} fusion(bf16[1024,256]{1,0:T(8,128)(2,1)} %param.11, s32[1024]{0:T(1024)S(1)} %broadcast_clamp_fusion), kind=kCustom, calls=%fused_computation | custom fusion | bytes 1052672 | tf_op jit(solution)/shard_map/gather | solution.py:47
  14.0 1.0 fusion.3
  15.0 0.8 copy-done.3
  16.2 1.7 scatter_custom_fusion
  18.0 21.1 %all-reduce.3.cloned.1.call-done = f32[256,256]{1,0:T(8,128)} async-done(((f32[256,256]{1,0:T(8,128)}), f32[256,256]{1,0:T(8,128)}) %all-reduce.3.cloned.1.call-update) | async-done | bytes 262160 | tf_op jit(solution)/shard_map/psum | solution.py:55
  39.1 6.0 %all_gather.3 = bf16[448,256]{0,1:T(8,128)(2,1)S(1)} all-gather(bf16[448,64]{0,1:T(8,128)(2,1)S(1)} %copy-done.7), channel_id=1, replica_groups=mesh['rec'=2,'leaf'=4,'rhs'=2,'pan'=2] {'rhs','pan'}, dimensions={1}, use_global_device_ids=true | all-gather | bytes 286720 | tf_op jit(solution)/shard_map/all_gather | solution.py:56
  45.4 0.8 fusion.45
  46.2 19.6 %all-reduce.5.cloned.1.call-done = f32[256,256]{1,0:T(8,128)} async-done(((f32[256,256]{1,0:T(8,128)}), f32[256,256]{1,0:T(8,128)}) %all-reduce.5.cloned.1.call-update) | async-done | bytes 262160 | tf_op jit(solution)/shard_map/psum | solution.py:55
  65.8 1.2 convolution_convert_fusion.1
  67.3 1.1 scatter_custom_fusion.1
  68.4 1.6 collective-permute-start
  70.1 6.0 %collective-permute-done = f32[256,256]{1,0:T(8,128)S(1)} collective-permute-done((f32[256,256]{1,0:T(8,128)S(1)}, f32[256,256]{1,0:T(8,128)S(1)}, u32[]{:S(2)}, u32[]{:S(2)}) %collective-permute-start) | collective-permute-done | bytes 262176 | tf_op jit(solution)/shard_map/ppermute | solution.py:10
  76.6 1.1 scatter_custom_fusion.2
  77.7 1.6 collective-permute-start.1
  79.2 5.2 %collective-permute-done.1 = f32[256,256]{1,0:T(8,128)S(1)} collective-permute-done((f32[256,256]{1,0:T(8,128)S(1)}, f32[256,256]{1,0:T(8,128)S(1)}, u32[]{:S(2)}, u32[]{:S(2)}) %collective-permute-start.1) | collective-permute-done | bytes 262176 | tf_op jit(solution)/shard_map/ppermute | solution.py:10
  84.5 2.5 %collective-permute-start.2 = (f32[256,256]{1,0:T(8,128)S(1)}, f32[256,256]{1,0:T(8,128)S(1)}, u32[]{:S(2)}, u32[]{:S(2)}) collective-permute-start(f32[256,256]{1,0:T(8,128)S(1)} %add.119), channel_id=1, source_target_pairs={{0,8},{4,12},{8,0},{12,4},{1,9},{5,13},{9,1},{13,5},{2,10},{6,14},... | collective-permute-start | bytes 786440 | tf_op jit(solution)/shard_map/ppermute | solution.py:10
  86.9 9.9 %collective-permute-done.2 = f32[256,256]{1,0:T(8,128)S(1)} collective-permute-done((f32[256,256]{1,0:T(8,128)S(1)}, f32[256,256]{1,0:T(8,128)S(1)}, u32[]{:S(2)}, u32[]{:S(2)}) %collective-permute-start.2) | collective-permute-done | bytes 262176 | tf_op jit(solution)/shard_map/ppermute | solution.py:10
  97.7 6.8 %collective-permute-done.3 = f32[256,256]{0,1:T(8,128)S(1)} collective-permute-done((f32[256,256]{0,1:T(8,128)S(1)}, f32[256,256]{0,1:T(8,128)S(1)}, u32[]{:S(2)}, u32[]{:S(2)}) %collective-permute-start.3) | collective-permute-done | bytes 262176 | tf_op jit(solution)/shard_map/ppermute | solution.py:10
  104.5 2.6 %collective-permute-start.4 = (f32[256,256]{0,1:T(8,128)S(1)}, f32[256,256]{0,1:T(8,128)S(1)}, u32[]{:S(2)}, u32[]{:S(2)}) collective-permute-start(f32[256,256]{0,1:T(8,128)S(1)} %add.121), channel_id=1, source_target_pairs={{0,8},{4,12},{8,0},{12,4},{1,9},{5,13},{9,1},{13,5},{2,10},{6,14},... | collective-permute-start | bytes 786440 | tf_op jit(solution)/shard_map/ppermute | solution.py:10
  107.1 10.9 %collective-permute-done.4 = f32[256,256]{0,1:T(8,128)S(1)} collective-permute-done((f32[256,256]{0,1:T(8,128)S(1)}, f32[256,256]{0,1:T(8,128)S(1)}, u32[]{:S(2)}, u32[]{:S(2)}) %collective-permute-start.4) | collective-permute-done | bytes 262176 | tf_op jit(solution)/shard_map/ppermute | solution.py:10
  118.1 0.8 gather_fusion.1
  119.3 0.8 collective-permute-start.5
  120.1 6.6 %collective-permute-done.5 = f32[256,256]{0,1:T(8,128)S(1)} collective-permute-done((f32[256,256]{0,1:T(8,128)S(1)}, f32[256,256]{0,1:T(8,128)S(1)}, u32[]{:S(2)}, u32[]{:S(2)}) %collective-permute-start.5) | collective-permute-done | bytes 262176 | tf_op jit(solution)/shard_map/ppermute | solution.py:10
  126.8 0.8 gather_fusion.2
  128.2 0.8 gather_fusion.3
  129.0 2.6 %fusion.4 = bf16[1024,256]{0,1:T(8,128)(2,1)} fusion(bf16[1024,1024]{1,0:T(8,128)(2,1)S(1)} %copy-done, bf16[128,256]{1,0:T(8,128)(2,1)S(1)} %gather_fusion.3, bf16[128,1024]{1,0:T(8,128)(2,1)} %param.13, bf16[256,1024]{1,0:T(8,128)(2,1)S(1)} %copy-done.4, f32[1024]{0:T(1024)S(1)} %get-tuple-element.11), kind=kOutput, calls=%fused_computation.15 | convolution fusion | flops 605552640 | bytes 3477504 | tf_op jit(solution)/shard_map/ij,ic->jc/dot_general | solution.py:111
  131.6 1.2 copy.36
  132.9 5.1 %scatter_custom_fusion.3 = bf16[1024,256]{1,0:T(8,128)(2,1)S(1)} fusion(s32[1024]{0:T(1024)S(1)} %bitcast.59, bf16[1024,256]{1,0:T(8,128)(2,1)S(1)} %copy.36, bf16[]{:T(256)} %constant.56.clone.1), kind=kCustom, calls=%fused_computation.42 | custom fusion | bytes 524290 | tf_op jit(solution)/shard_map/scatter | solution.py:114
  138.0 1.9 fusion.5
  139.9 1.0 copy.38
  140.9 57.0 %reduce-scatter.4.cloned.1.call-done = f32[32,256]{1,0:T(8,128)} async-done(((f32[512,256]{1,0:T(8,128)}), f32[32,256]{1,0:T(8,128)}) %reduce-scatter.4.cloned.1.call-update) | async-done | bytes 32784
  (53 shorter events, 4.5 us)
Async XLA Ops:
  7.2 6.8 %copy-start = (bf16[1024,1024]{1,0:T(8,128)(2,1)S(1)}, bf16[1024,1024]{1,0:T(8,128)(2,1)}, u32[]{:S(2)}) copy-start(bf16[1024,1024]{1,0:T(8,128)(2,1)} %param.12) | copy-start | bytes 6291460
  7.2 31.9 %all-reduce.3.cloned.1.call-start = ((), (), s32[]{:S(2)}) async-start(), calls=%async_computation.1 | async-start | bytes 524288 | tf_op jit(solution)/shard_map/psum | solution.py:55
  14.0 1.8 copy-start.6
  14.0 25.2 %copy-start.7 = (bf16[448,64]{0,1:T(8,128)(2,1)S(1)}, bf16[448,64]{0,1:T(8,128)(2,1)}, u32[]{:S(2)}) copy-start(bf16[448,64]{0,1:T(8,128)(2,1)} %param.18) | copy-start | bytes 172036
  15.0 0.8 copy-start.3
  15.8 50.0 %copy-start.2 = (bf16[448,256]{1,0:T(8,128)(2,1)S(1)}, bf16[448,256]{1,0:T(8,128)(2,1)}, u32[]{:S(2)}) copy-start(bf16[448,256]{1,0:T(8,128)(2,1)} %param.19) | copy-start | bytes 688132
  15.8 51.2 %copy-start.5 = (bf16[128,384]{1,0:T(8,128)(2,1)S(1)}, bf16[128,384]{1,0:T(8,128)(2,1)}, u32[]{:S(2)}) copy-start(bf16[128,384]{1,0:T(8,128)(2,1)} %param.20) | copy-start | bytes 294916
  17.9 47.9 %all-reduce.5.cloned.1.call-start = ((), (), s32[]{:S(2)}) async-start(), calls=%async_computation.2 | async-start | bytes 524288 | tf_op jit(solution)/shard_map/psum | solution.py:55
  39.1 158.8 %reduce-scatter.4.cloned.1.call-start = ((), (), s32[]{:S(2)}) async-start(), calls=%async_computation.3 | async-start | bytes 557056
  68.4 7.7 %collective-permute-start = (f32[256,256]{1,0:T(8,128)S(1)}, f32[256,256]{1,0:T(8,128)S(1)}, u32[]{:S(2)}, u32[]{:S(2)}) collective-permute-start(f32[256,256]{1,0:T(8,128)S(1)} %add_dynamic-update-slice_fusion), channel_id=1, source_target_pairs={{0,4},{4,0},{8,12},{12,8},{1,5},{5,1},{9,13},{13,9},{2,6},{6,2},{1... | collective-permute-start | bytes 786440 | tf_op jit(solution)/shard_map/ppermute | solution.py:10
  77.7 6.7 %collective-permute-start.1 = (f32[256,256]{1,0:T(8,128)S(1)}, f32[256,256]{1,0:T(8,128)S(1)}, u32[]{:S(2)}, u32[]{:S(2)}) collective-permute-start(f32[256,256]{1,0:T(8,128)S(1)} %add_dynamic-update-slice_fusion.1), channel_id=1, source_target_pairs={{0,4},{4,0},{8,12},{12,8},{1,5},{5,1},{9,13},{13,9},{2,6},{6,2},{1... | collective-permute-start | bytes 786440 | tf_op jit(solution)/shard_map/ppermute | solution.py:10
  84.5 12.3 %collective-permute-start.2 = (f32[256,256]{1,0:T(8,128)S(1)}, f32[256,256]{1,0:T(8,128)S(1)}, u32[]{:S(2)}, u32[]{:S(2)}) collective-permute-start(f32[256,256]{1,0:T(8,128)S(1)} %add.119), channel_id=1, source_target_pairs={{0,8},{4,12},{8,0},{12,4},{1,9},{5,13},{9,1},{13,5},{2,10},{6,14},... | collective-permute-start | bytes 786440 | tf_op jit(solution)/shard_map/ppermute | solution.py:10
  97.2 7.3 %collective-permute-start.3 = (f32[256,256]{0,1:T(8,128)S(1)}, f32[256,256]{0,1:T(8,128)S(1)}, u32[]{:S(2)}, u32[]{:S(2)}) collective-permute-start(f32[256,256]{0,1:T(8,128)S(1)} %convolution_bitcast_fusion.1), channel_id=1, source_target_pairs={{0,4},{4,0},{8,12},{12,8},{1,5},{5,1},{9,13},{13,9},{2,6},{6,2},{1... | collective-permute-start | bytes 786440 | tf_op jit(solution)/shard_map/ppermute | solution.py:10
  104.5 13.5 %collective-permute-start.4 = (f32[256,256]{0,1:T(8,128)S(1)}, f32[256,256]{0,1:T(8,128)S(1)}, u32[]{:S(2)}, u32[]{:S(2)}) collective-permute-start(f32[256,256]{0,1:T(8,128)S(1)} %add.121), channel_id=1, source_target_pairs={{0,8},{4,12},{8,0},{12,4},{1,9},{5,13},{9,1},{13,5},{2,10},{6,14},... | collective-permute-start | bytes 786440 | tf_op jit(solution)/shard_map/ppermute | solution.py:10
  118.0 11.0 %copy-start.4 = (bf16[256,1024]{1,0:T(8,128)(2,1)S(1)}, bf16[256,1024]{1,0:T(8,128)(2,1)}, u32[]{:S(2)}) copy-start(bf16[256,1024]{1,0:T(8,128)(2,1)} %copy-done.3) | copy-start | bytes 1572868
  119.3 7.4 %collective-permute-start.5 = (f32[256,256]{0,1:T(8,128)S(1)}, f32[256,256]{0,1:T(8,128)S(1)}, u32[]{:S(2)}, u32[]{:S(2)}) collective-permute-start(f32[256,256]{0,1:T(8,128)S(1)} %convolution_bitcast_fusion), channel_id=1, source_target_pairs={{0,4},{4,0},{8,12},{12,8},{1,5},{5,1},{9,13},{13,9},{2,6},{6,2},{1... | collective-permute-start | bytes 786440 | tf_op jit(solution)/shard_map/ppermute | solution.py:10
  138.0 60.0 %copy-start.1 = (bf16[1024,256]{1,0:T(8,128)(2,1)}, bf16[1024,256]{1,0:T(8,128)(2,1)S(1)}, u32[]{:S(2)}) copy-start(bf16[1024,256]{1,0:T(8,128)(2,1)S(1)} %scatter_custom_fusion.3) | copy-start | bytes 1572868
Sparse Core Ops, SparseCore 0:
  18.1 20.9 all-reduce.2
  41.4 24.3 all-reduce.4
  141.0 56.8 reduce-scatter.3
